TPU v7x, 32 devices: a whole 2x2x4 slice. The times are simulated.
32 devices in a mesh: scen: 4 (over z), net: 8 (over y, x, core).
Axes of the slice: x: 2, y: 2, z: 4, core: 2. Of those that a mesh axis runs over, the one named last changes fastest.
Arguments:
- coupling: bfloat16 [768, 64, 320], P('net'), may hold values from -0.3125 to 0.3125
- tie_blocks: bfloat16 [1024, 64, 128], P('net'), may hold values from -0.5 to 0.5
- w_pattern: int32 [768, 4], P('net'), may hold values from 0 to 127
- link_pattern: int32 [768], P('net'), may hold values from 0 to 127
- left_bounds: int32 [1024], P('net'), may hold values from 0 to 127
- right_bounds: int32 [1024], P('net'), may hold values from 0 to 127
- block_counts: int32 [8], P('net'), may hold values from 48 to 96, as said below
- commit_cost: float32 [1024, 64], P('net'), may hold values from -3 to 3
- dispatch_cost: float32 [1024, 64], P('net'), may hold values from -6 to 6
- demand: float32 [768, 64], P('net'), may hold values from -6 to 6
- wind_error: bfloat16 [768, 64, 512], P('net', None, 'scen'), may hold values from -3 to 3
- commit_start: float32 [1024, 64], P('net'), may hold values from 0 to 1
- dispatch_start: float32 [1024, 64, 512], P('net', None, 'scen'), may hold values from 0 to 2
- dual_start: float32 [768, 64, 512], P('net', None, 'scen'), may hold values from -8 to 8
- tie_start: float32 [1024, 64, 512], P('net', None, 'scen'), may hold values from -6 to 6
Outputs:
- commit_out: float32 [1024, 64], P('net')
- dispatch_out: float32 [1024, 64, 512], P('net', None, 'scen')
- dual_out: float32 [768, 64, 512], P('net', None, 'scen')
- tie_out: float32 [1024, 64, 512], P('net', None, 'scen')
Inputs may be any that keep to these rules, and one draw needn't show every extreme that they name: `block_counts`: some partition has all 96 row blocks active.
All inputs are finite; a program needn't handle non-finite values.
Results may differ from a plain program's by a relative error of at most 0.0035.
Values may be sent and summed in bfloat16 or wider, within the bound.
A program may use at most 192 MiB of HBM per device.

v0:
```python
import jax
import jax.numpy as jnp
from jax import lax
from jax.sharding import PartitionSpec as P

BLK = 64
KW = 4
ITERS = 2
YB = 128
XB = 128
primal_step = 0.4
first_step = 1.0
dual_step = 0.4


def from_behind(value, axis, by):
    devices = lax.axis_size(axis)
    pairs = [(i, i + by) for i in range(devices) if 0 <= i + by < devices]
    return lax.ppermute(value, axis, pairs)


def apply_blocks(block_mats, stacked):
    return jnp.einsum("roj,rjs->ros", block_mats, stacked, preferred_element_type=jnp.float32)


def transpose_blocks(block_mats, dual_rows):
    return jnp.einsum("roj,ros->rjs", block_mats, dual_rows, preferred_element_type=jnp.float32)


def one_hot_rows(indices, count):
    return (indices[None, :] == jnp.arange(count, dtype=jnp.int32)[:, None]).astype(jnp.float32)


def sum_into(selector, terms):
    return jnp.einsum(
        "bk,kos->bos",
        selector,
        terms,
        precision=lax.Precision.HIGHEST,
        preferred_element_type=jnp.float32,
    )


def body(
    coupling,
    tie_blocks,
    w_pattern,
    link_pattern,
    left_bounds,
    right_bounds,
    block_counts,
    commit_cost,
    dispatch_cost,
    demand,
    wind_error,
    commit_start,
    dispatch_start,
    dual_start,
    tie_start,
):
    row_count = coupling.shape[0]
    scen_dev = dispatch_start.shape[2]
    scen_total = scen_dev * lax.axis_size("scen")
    lead = KW * BLK
    live_tie = (lax.axis_index("net") < lax.axis_size("net") - 1).astype(jnp.float32)
    active = (jnp.arange(row_count) < block_counts[0]).astype(jnp.float32)[:, None, None]
    pattern_select = one_hot_rows(w_pattern.reshape(-1), YB)
    link_select = one_hot_rows(link_pattern, XB)
    right_select = one_hot_rows(right_bounds, YB)
    left_select = one_hot_rows(left_bounds, YB)
    recourse = coupling[:, :, :lead]
    linking = coupling[:, :, lead:]
    cost_col = dispatch_cost[:, :, None]
    target = demand[:, :, None] + wind_error.astype(jnp.float32)
    first_now = commit_start
    second_now = dispatch_start
    dual_now = dual_start * active
    tie_now = tie_start * live_tie
    for iteration in range(ITERS):
        dual_half = dual_now.astype(jnp.bfloat16)
        tie_half = tie_now.astype(jnp.bfloat16)
        recourse_terms = transpose_blocks(recourse, dual_half).reshape(
            row_count * KW, BLK, scen_dev
        )
        grad_second = sum_into(pattern_select, recourse_terms)
        link_terms = (
            jnp.einsum("roj,ros->rj", linking, dual_half, preferred_element_type=jnp.float32)
            / scen_total
        )
        grad_part = jnp.dot(
            link_select,
            link_terms,
            precision=lax.Precision.HIGHEST,
            preferred_element_type=jnp.float32,
        )
        tie_terms = transpose_blocks(tie_blocks, tie_half)
        own_terms = tie_terms[:, :BLK]
        left_terms = from_behind(tie_terms[:, BLK:], "net", 1)
        grad_second = grad_second + sum_into(right_select, own_terms)
        grad_second = grad_second + sum_into(left_select, left_terms)
        grad_first = lax.psum(grad_part.astype(jnp.bfloat16), "scen").astype(jnp.float32)
        first_next = jnp.clip(first_now - first_step * (commit_cost - grad_first), 0.0, 1.0)
        second_next = jnp.maximum(second_now - primal_step * (cost_col - grad_second), 0.0)
        first_bar = (2.0 * first_next - first_now).astype(jnp.bfloat16)
        second_bar = (2.0 * second_next - second_now).astype(jnp.bfloat16)
        next_rows = from_behind(second_bar[left_bounds], "net", -1)
        tie_inputs = jnp.concatenate([second_bar[right_bounds], next_rows], axis=1)
        tie_rows = apply_blocks(tie_blocks, tie_inputs)
        gathered = second_bar[w_pattern].reshape(row_count, lead, scen_dev)
        linked = jnp.einsum(
            "roi,ri->ro", linking, first_bar[link_pattern], preferred_element_type=jnp.float32
        )
        coupled = apply_blocks(recourse, gathered) + linked[:, :, None]
        dual_now = (dual_now + dual_step * (target - coupled)) * active
        tie_now = (tie_now - dual_step * tie_rows) * live_tie
        first_now = first_next
        second_now = second_next
    return (first_now, second_now, dual_now, tie_now)


def solution(mesh):
    return jax.shard_map(
        body,
        mesh=mesh,
        in_specs=(
            P("net", None, None),
            P("net", None, None),
            P("net", None),
            P("net"),
            P("net"),
            P("net"),
            P("net"),
            P("net", None),
            P("net", None),
            P("net", None),
            P("net", None, "scen"),
            P("net", None),
            P("net", None, "scen"),
            P("net", None, "scen"),
            P("net", None, "scen"),
        ),
        out_specs=(
            P("net", None),
            P("net", None, "scen"),
            P("net", None, "scen"),
            P("net", None, "scen"),
        ),
        check_vma=False,
    )
```

profile of v0, /device:TPU:0, one launch (start us, length us, event | category | flops | bytes accessed | tf_op | source)
XLA Modules:
  0.0 271.5 jit_solution(8567158418583271729)
XLA Ops:
  0.6 0.0 copy-start
  0.7 1.6 copy-done
  2.2 3.7 %convolution_bitcast_fusion.3 = f32[128,128,128]{2,1,0:T(8,128)S(1)} fusion(bf16[128,64,128]{2,1,0:T(8,128)(2,1)S(1)} %copy-done, f32[128,64,128]{2,1,0:T(8,128)} %param.29, f32[]{:T(128)S(6)} %convert_element_type.65), kind=kOutput, calls=%fused_computation.40 | convolution fusion | flops 270532608 | bytes 14680068 | tf_op jit(solution)/shard_map/roj,ros->rjs/dot_general | solution.py:27
  5.9 0.0 slice-start.1
  5.9 0.0 copy-start.5
  5.9 4.3 %fusion.85 = (f32[128,64,128]{2,1,0:T(8,128)}, f32[128,64,128]{2,1,0:T(8,128)}) fusion(f32[128,128,128]{2,1,0:T(8,128)S(1)} %convolution_bitcast_fusion.3), kind=kLoop, calls=%fused_computation.111 | loop fusion | bytes 16777216 | tf_op jit(solution)/shard_map/slice | solution.py:98
  10.2 4.3 %collective-permute-start = (f32[128,64,128]{2,1,0:T(8,128)}, f32[128,64,128]{2,1,0:T(8,128)}, u32[]{:S(2)}, u32[]{:S(2)}) collective-permute-start(f32[128,64,128]{2,1,0:T(8,128)} %get-tuple-element.16), channel_id=1, source_target_pairs={{0,1},{1,2},{2,3},{3,4},{4,5},{5,6},{6,7},{8,9},{9,10},{10,11},{11... | collective-permute-start | bytes 12582920 | tf_op jit(solution)/shard_map/ppermute | solution.py:19
  15.2 6.9 %convolution_bitcast_fusion.1 = f32[96,256,128]{1,2,0:T(8,128)} fusion(bf16[96,64,320]{2,1,0:T(8,128)(2,1)S(1)} %bitcast.81, f32[96,64,128]{2,1,0:T(8,128)S(1)} %copy-done.5, f32[96]{0:T(128)S(1)} %compare_convert_fusion), kind=kOutput, calls=%fused_computation.13 | convolution fusion | flops 404226048 | bytes 18874880 | tf_op jit(solution)/shard_map/roj,ros->rjs/dot_general | solution.py:27
  22.1 12.8 %copy.33 = f32[96,256,128]{2,1,0:T(8,128)} copy(f32[96,256,128]{1,2,0:T(8,128)} %convolution_bitcast_fusion.1) | data formatting | bytes 25165824 | tf_op jit(solution)/shard_map/roj,ros->rjs/dot_general | solution.py:27
  35.0 0.1 copy.32
  35.1 0.1 eq.57
  35.2 6.7 %fusion.20 = f32[128,64,128]{2,0,1:T(8,128)S(1)} fusion(f32[128,64,128]{2,1,0:T(8,128)} %get-tuple-element.17, s32[128]{0:T(128)S(1)} %copy-done.16), kind=kOutput, calls=%fused_computation.32 | convolution fusion | flops 1610629120 | bytes 8389120 | tf_op jit(solution)/shard_map/bk,kos->bos/dot_general | solution.py:35
  41.9 0.0 copy-start.9
  41.9 0.0 copy-start.10
  41.9 16.6 %fusion.2 = f32[128,64,128]{2,0,1:T(8,128)S(1)} fusion(f32[384,64,128]{2,1,0:T(8,128)} %bitcast.78, s32[384]{0:T(512)S(1)} %eq.57), kind=kOutput, calls=%fused_computation.10 | convolution fusion | flops 4831887360 | bytes 16778752 | tf_op jit(solution)/shard_map/bk,kos->bos/dot_general | solution.py:35
  58.6 13.5 %subtract_convert_fusion.1 = (bf16[128,64,128]{2,0,1:T(8,128)(2,1)S(1)}, f32[128,64,128]{2,0,1:T(8,128)}) fusion(f32[128,64,128]{2,1,0:T(8,128)S(1)} %copy-done.9, f32[128,64,128]{2,1,0:T(8,128)} %collective-permute-done, s32[128]{0:T(128)S(1)} %copy-done.15, f32[128,64,128]{2,0,1:T(8,128)S(1)} %fusion.2, f32[128,64,128]{2,0,1:T(8,128)S(1)} %fusion.20, ...), kind=kOutput, calls=%fused_computation.36 | convolution fusion | flops 1620066304 | bytes 23101952 | tf_op jit(solution)/shard_map/bk,kos->bos/dot_general | solution.py:35
  72.1 2.7 copy.40
  74.7 3.7 %gather_fusion.3 = bf16[128,64,128]{2,1,0:T(8,128)(2,1)} fusion(bf16[128,64,128]{2,1,0:T(8,128)(2,1)} %copy.40, s32[1024]{0:T(1024)S(1)} %pad_clamp_fusion), kind=kCustom, calls=%fused_computation.3 | custom fusion | bytes 4194816 | tf_op jit(solution)/shard_map/gather | solution.py:106
  78.5 1.3 collective-permute-start.1
  79.8 2.9 %convert_reduce_fusion.1 = f32[96,64]{1,0:T(8,128)S(1)} fusion(f32[96,64,128]{2,1,0:T(8,128)} %param.28, f32[96]{0:T(128)S(1)} %compare_convert_fusion), kind=kLoop, calls=%fused_computation.51 | loop fusion | flops 3139584 | bytes 3170688 | tf_op jit(solution)/shard_map/roj,ros->rj/reduce_sum | solution.py:87
  82.7 3.7 %gather_fusion.2 = bf16[128,64,128]{2,1,0:T(8,128)(2,1)} fusion(bf16[128,64,128]{2,1,0:T(8,128)(2,1)} %copy.40, s32[1024]{0:T(1024)S(1)} %pad_clamp_fusion.1), kind=kCustom, calls=%fused_computation.2 | custom fusion | bytes 4194816 | tf_op jit(solution)/shard_map/gather | solution.py:107
  86.4 0.3 collective-permute-done.1
  86.7 4.7 %fusion.13 = f32[128,64,128]{2,1,0:T(8,128)S(1)} fusion(f32[128,64,128]{2,1,0:T(8,128)} %param.29, bf16[128,64,128]{2,1,0:T(8,128)(2,1)S(1)} %copy-done, bf16[128,64,128]{2,1,0:T(8,128)(2,1)} %collective-permute-done.1, bf16[128,64,128]{2,1,0:T(8,128)(2,1)} %gather_fusion.2, f32[]{:T(128)S(6)} %convert_element_type.65), kind=kOutput, calls=%fused_computation.25 | convolution fusion | flops 281018368 | bytes 14680068 | tf_op jit(solution)/shard_map/roj,rjs->ros/dot_general | solution.py:23
  91.4 2.0 copy-done.1
  93.3 1.3 convolution_bitcast_fusion.2
  94.7 0.0 copy-start.17
  94.7 0.0 copy-start.11
  94.7 0.0 copy-start.12
  94.7 4.2 %fusion.84 = (f32[128,64,128]{2,1,0:T(8,128)}, f32[128,64,128]{2,1,0:T(8,128)}) fusion(f32[128,128,128]{2,1,0:T(8,128)S(1)} %convolution_bitcast_fusion.2), kind=kLoop, calls=%fused_computation.110 | loop fusion | bytes 16777216 | tf_op jit(solution)/shard_map/slice | solution.py:98
  98.9 26.5 %collective-permute-start.2 = (f32[128,64,128]{2,1,0:T(8,128)}, f32[128,64,128]{2,1,0:T(8,128)}, u32[]{:S(2)}, u32[]{:S(2)}) collective-permute-start(f32[128,64,128]{2,1,0:T(8,128)} %get-tuple-element.14), channel_id=1, source_target_pairs={{0,1},{1,2},{2,3},{3,4},{4,5},{5,6},{6,7},{8,9},{9,10},{10,11},{11... | collective-permute-start | bytes 12582920 | tf_op jit(solution)/shard_map/ppermute | solution.py:19
  125.4 1.9 fusion.54
  127.4 0.2 convolution_convert_fusion.1
  127.6 19.2 %psum.14 = bf16[128,64]{0,1:T(8,128)(2,1)S(1)} all-reduce(bf16[128,64]{0,1:T(8,128)(2,1)S(1)} %convolution_convert_fusion.1), channel_id=1, replica_groups=mesh['scen'=4,'net'=8] {'scen'}, use_global_device_ids=true, to_apply=%region_1.0 | all-reduce | flops 8192 | bytes 32768 | tf_op jit(solution)/shard_map/psum | solution.py:101
  146.9 0.1 copy.41
  147.0 0.1 copy.39
  147.1 0.1 reshape.39
  147.2 0.1 copy.31
  147.4 0.7 gather_fusion.1
  148.0 2.3 fusion.52
  150.4 5.7 %gather_fusion = bf16[384,64,128]{2,1,0:T(8,128)(2,1)} fusion(bf16[128,64,128]{2,1,0:T(8,128)(2,1)} %copy.40, s32[1024]{0:T(1024)S(1)} %pad_clamp_fusion.3), kind=kCustom, calls=%fused_computation | custom fusion | bytes 12584448 | tf_op jit(solution)/shard_map/gather | solution.py:109
  156.0 6.8 %convert_reduce_fusion = (f32[96,64]{1,0:T(8,128)S(1)}, f32[96,64,128]{2,1,0:T(8,128)S(1)}) fusion(f32[96,64]{1,0:T(8,128)S(1)} %bitcast.93, bf16[96,256,128]{2,1,0:T(8,128)(2,1)} %bitcast.87, bf16[96,64,320]{2,1,0:T(8,128)(2,1)} %param.15, bf16[96,64,128]{2,1,0:T(8,128)(2,1)} %param.25, f32[96,64]{1,0:T(8,128)S(1)} %copy.31, f32[96,64,128]{2,1,0:T(8,128)} %param.28, ...), kind=kOutput, calls=%fused_computation.49 | convolution fusion | flops 411297792 | bytes 17375616 | tf_op jit(solution)/shard_map/roj,rjs->ros/dot_general | solution.py:23
  162.8 1.7 copy-done.3
  164.5 6.4 %convolution_bitcast_fusion = f32[96,256,128]{1,2,0:T(8,128)} fusion(bf16[96,64,320]{2,1,0:T(8,128)(2,1)S(1)} %bitcast.83, f32[96,64,128]{2,1,0:T(8,128)S(1)} %get-tuple-element.21), kind=kOutput, calls=%fused_computation.12 | convolution fusion | flops 403439616 | bytes 18874368 | tf_op jit(solution)/shard_map/roj,ros->rjs/dot_general | solution.py:27
  170.9 12.6 %copy.42 = f32[96,256,128]{2,1,0:T(8,128)} copy(f32[96,256,128]{1,2,0:T(8,128)} %convolution_bitcast_fusion) | data formatting | bytes 25165824 | tf_op jit(solution)/shard_map/roj,ros->rjs/dot_general | solution.py:27
  183.5 16.6 %fusion = f32[128,64,128]{2,0,1:T(8,128)S(1)} fusion(f32[384,64,128]{2,1,0:T(8,128)} %bitcast.79, s32[384]{0:T(512)S(1)} %eq.57), kind=kOutput, calls=%fused_computation.8 | convolution fusion | flops 4831887360 | bytes 16778752 | tf_op jit(solution)/shard_map/bk,kos->bos/dot_general | solution.py:35
  200.1 0.0 copy-start.6
  200.1 4.7 %fusion.16 = f32[128,64,128]{2,0,1:T(8,128)S(1)} fusion(f32[128,64,128]{2,1,0:T(8,128)S(1)} %copy-done.7, s32[128]{0:T(128)S(1)} %copy-done.16), kind=kOutput, calls=%fused_computation.28 | convolution fusion | flops 1610629120 | bytes 8389120 | tf_op jit(solution)/shard_map/bk,kos->bos/dot_general | solution.py:35
  204.8 9.8 %subtract_convert_fusion = (bf16[128,64,128]{2,0,1:T(8,128)(2,1)S(1)}, f32[128,64,128]{2,0,1:T(8,128)}) fusion(f32[128,64,128]{2,0,1:T(8,128)S(1)} %copy-done.6, f32[128,64,128]{2,1,0:T(8,128)} %collective-permute-done.2, s32[128]{0:T(128)S(1)} %copy-done.15, f32[128,64,128]{2,0,1:T(8,128)S(1)} %fusion, f32[128,64,128]{2,0,1:T(8,128)S(1)} %fusion.16, ...), kind=kOutput, calls=%fused_computation.34 | convolution fusion | flops 1620066304 | bytes 23101952 | tf_op jit(solution)/shard_map/bk,kos->bos/dot_general | solution.py:35
  214.6 2.7 copy.48
  217.3 3.8 %gather_fusion.7 = bf16[128,64,128]{2,1,0:T(8,128)(2,1)} fusion(bf16[128,64,128]{2,1,0:T(8,128)(2,1)} %copy.48, s32[1024]{0:T(1024)S(1)} %pad_clamp_fusion), kind=kCustom, calls=%fused_computation.7 | custom fusion | bytes 4194816 | tf_op jit(solution)/shard_map/gather | solution.py:106
  221.1 1.3 collective-permute-start.3
  222.4 1.9 fusion.50
  224.3 0.2 convolution_convert_fusion
  224.6 15.5 %psum.15 = bf16[128,64]{0,1:T(8,128)(2,1)S(1)} all-reduce(bf16[128,64]{0,1:T(8,128)(2,1)S(1)} %convolution_convert_fusion), channel_id=1, replica_groups=mesh['scen'=4,'net'=8] {'scen'}, use_global_device_ids=true, to_apply=%region_3.4 | all-reduce | flops 8192 | bytes 32768 | tf_op jit(solution)/shard_map/psum | solution.py:101
  240.1 0.6 subtract_convert_fusion.2
  240.7 0.1 copy.49
  240.8 0.7 gather_fusion.5
  241.5 2.3 fusion.48
  243.8 5.6 %gather_fusion.4 = bf16[384,64,128]{2,1,0:T(8,128)(2,1)} fusion(bf16[128,64,128]{2,1,0:T(8,128)(2,1)} %copy.48, s32[1024]{0:T(1024)S(1)} %pad_clamp_fusion.3), kind=kCustom, calls=%fused_computation.4 | custom fusion | bytes 12584448 | tf_op jit(solution)/shard_map/gather | solution.py:109
  249.5 3.8 %gather_fusion.6 = bf16[128,64,128]{2,1,0:T(8,128)(2,1)} fusion(bf16[128,64,128]{2,1,0:T(8,128)(2,1)} %copy.48, s32[1024]{0:T(1024)S(1)} %pad_clamp_fusion.1), kind=kCustom, calls=%fused_computation.6 | custom fusion | bytes 4194816 | tf_op jit(solution)/shard_map/gather | solution.py:107
  253.3 6.8 %copy.52 = f32[128,64,128]{2,1,0:T(8,128)} copy(f32[128,64,128]{2,0,1:T(8,128)} %get-tuple-element.23) | data formatting | bytes 8388608
  260.1 5.5 %fusion.24 = f32[96,64,128]{2,1,0:T(8,128)} fusion(f32[96,64,128]{2,1,0:T(8,128)S(1)} %copy-done.4, bf16[96,64,128]{2,1,0:T(8,128)(2,1)} %param.25, bf16[96,256,128]{2,1,0:T(8,128)(2,1)} %bitcast.86, bf16[96,64,320]{2,1,0:T(8,128)(2,1)S(1)} %bitcast.85, f32[96,64]{1,0:T(8,128)S(1)} %bitcast.88, f32[96,64]{1,0:T(8,128)S(1)} %copy.31, ...), kind=kOutput, calls=%fused_computation.44 | convolution fusion | flops 408158208 | bytes 17400320 | tf_op jit(solution)/shard_map/roj,rjs->ros/dot_general | solution.py:23
  265.6 0.7 copy-done.8
  266.4 4.9 %fusion.12 = f32[128,64,128]{2,1,0:T(8,128)} fusion(f32[128,64,128]{2,1,0:T(8,128)S(1)} %copy-done.2, bf16[128,64,128]{2,1,0:T(8,128)(2,1)S(1)} %copy-done, bf16[128,64,128]{2,1,0:T(8,128)(2,1)} %collective-permute-done.3, bf16[128,64,128]{2,1,0:T(8,128)(2,1)S(1)} %copy-done.8, f32[]{:T(128)S(6)} %convert_element_type.65), kind=kOutput, calls=%fused_computation.23 | convolution fusion | flops 279969792 | bytes 14680068 | tf_op jit(solution)/shard_map/roj,rjs->ros/dot_general | solution.py:23
  (51 shorter events, 0.1 us)
Async XLA Ops:
  0.6 1.6 copy-start
  2.2 13.0 %slice-start = ((s8[4718592]{0:T(1024)(128)(4,1)}), s8[4194304]{0:T(1024)(128)(4,1)S(1)}, s32[]{:S(2)}) async-start(s8[4718592]{0:T(1024)(128)(4,1)} %bitcast.80), calls=%async_computation | async-start | bytes 8388608
  5.9 9.3 %slice-start.1 = ((s8[4718592]{0:T(1024)(128)(4,1)}), s8[524288]{0:T(1024)(128)(4,1)S(1)}, s32[]{:S(2)}) async-start(s8[4718592]{0:T(1024)(128)(4,1)} %bitcast.80), calls=%async_computation.1 | async-start | bytes 1048576
  5.9 9.3 %copy-start.5 = (f32[96,64,128]{2,1,0:T(8,128)S(1)}, f32[96,64,128]{2,1,0:T(8,128)}, u32[]{:S(2)}) copy-start(f32[96,64,128]{2,1,0:T(8,128)} %param.28) | copy-start | bytes 9437188
  10.2 48.3 %collective-permute-start = (f32[128,64,128]{2,1,0:T(8,128)}, f32[128,64,128]{2,1,0:T(8,128)}, u32[]{:S(2)}, u32[]{:S(2)}) collective-permute-start(f32[128,64,128]{2,1,0:T(8,128)} %get-tuple-element.16), channel_id=1, source_target_pairs={{0,1},{1,2},{2,3},{3,4},{4,5},{5,6},{6,7},{8,9},{9,10},{10,11},{11... | collective-permute-start | bytes 12582920 | tf_op jit(solution)/shard_map/ppermute | solution.py:19
  22.1 12.8 %copy-start.14 = (s32[96,4]{0,1:T(4,128)S(1)}, s32[96,4]{0,1:T(4,128)}, u32[]{:S(2)}) copy-start(s32[96,4]{0,1:T(4,128)} %param.17) | copy-start | bytes 4612
  22.1 13.0 %copy-start.15 = (s32[128]{0:T(128)S(1)}, s32[128]{0:T(128)}, u32[]{:S(2)}) copy-start(s32[128]{0:T(128)} %param.19) | copy-start | bytes 1540
  22.1 13.1 %copy-start.16 = (s32[128]{0:T(128)S(1)}, s32[128]{0:T(128)}, u32[]{:S(2)}) copy-start(s32[128]{0:T(128)} %param.20) | copy-start | bytes 1540
  41.9 16.7 %copy-start.9 = (f32[128,64,128]{2,1,0:T(8,128)S(1)}, f32[128,64,128]{2,1,0:T(8,128)}, u32[]{:S(2)}) copy-start(f32[128,64,128]{2,1,0:T(8,128)} %param.27) | copy-start | bytes 12582916
  41.9 16.7 %copy-start.10 = (f32[128,64]{0,1:T(8,128)S(1)}, f32[128,64]{0,1:T(8,128)}, u32[]{:S(2)}) copy-start(f32[128,64]{0,1:T(8,128)} %param.23) | copy-start | bytes 98308
  78.5 8.2 %collective-permute-start.1 = (bf16[128,64,128]{2,1,0:T(8,128)(2,1)}, bf16[128,64,128]{2,1,0:T(8,128)(2,1)}, u32[]{:S(2)}, u32[]{:S(2)}) collective-permute-start(bf16[128,64,128]{2,1,0:T(8,128)(2,1)} %gather_fusion.3), channel_id=1, source_target_pairs={{1,0},{2,1},{3,2},{4,3},{5,4},{6,5},{7,6},{9,8},{10,9},{11,10},{12... | collective-permute-start | bytes 6291464 | tf_op jit(solution)/shard_map/ppermute | solution.py:19
  91.4 2.0 copy-start.1
  94.7 32.7 %copy-start.17 = (s32[96]{0:T(128)S(1)}, s32[96]{0:T(128)}, u32[]{:S(2)}) copy-start(s32[96]{0:T(128)} %param.18) | copy-start | bytes 1156
  94.7 52.2 %copy-start.11 = (f32[128,64]{0,1:T(8,128)S(1)}, f32[128,64]{0,1:T(8,128)}, u32[]{:S(2)}) copy-start(f32[128,64]{0,1:T(8,128)} %param.26) | copy-start | bytes 98308
  94.7 52.2 %copy-start.12 = (f32[128,64]{0,1:T(8,128)S(1)}, f32[128,64]{0,1:T(8,128)}, u32[]{:S(2)}) copy-start(f32[128,64]{0,1:T(8,128)} %param.22) | copy-start | bytes 98308
  94.7 52.5 %copy-start.13 = (f32[96,64]{0,1:T(8,128)S(1)}, f32[96,64]{0,1:T(8,128)}, u32[]{:S(2)}) copy-start(f32[96,64]{0,1:T(8,128)} %param.24) | copy-start | bytes 73732
  98.9 105.9 %collective-permute-start.2 = (f32[128,64,128]{2,1,0:T(8,128)}, f32[128,64,128]{2,1,0:T(8,128)}, u32[]{:S(2)}, u32[]{:S(2)}) collective-permute-start(f32[128,64,128]{2,1,0:T(8,128)} %get-tuple-element.14), channel_id=1, source_target_pairs={{0,1},{1,2},{2,3},{3,4},{4,5},{5,6},{6,7},{8,9},{9,10},{10,11},{11... | collective-permute-start | bytes 12582920 | tf_op jit(solution)/shard_map/ppermute | solution.py:19
  150.3 14.1 %slice-start.2 = ((s8[4718592]{0:T(1024)(128)(4,1)}), s8[524288]{0:T(1024)(128)(4,1)S(1)}, s32[]{:S(2)}) async-start(s8[4718592]{0:T(1024)(128)(4,1)} %bitcast.82), calls=%async_computation.2 | async-start | bytes 1048576
  156.0 8.4 %slice-start.3 = ((s8[4718592]{0:T(1024)(128)(4,1)}), s8[4194304]{0:T(1024)(128)(4,1)S(1)}, s32[]{:S(2)}) async-start(s8[4718592]{0:T(1024)(128)(4,1)} %bitcast.82), calls=%async_computation.3 | async-start | bytes 8388608
  162.8 1.7 copy-start.3
  183.5 16.6 %copy-start.7 = (f32[128,64,128]{2,1,0:T(8,128)S(1)}, f32[128,64,128]{2,1,0:T(8,128)}, u32[]{:S(2)}) copy-start(f32[128,64,128]{2,1,0:T(8,128)} %get-tuple-element.15) | copy-start | bytes 12582916
  200.1 4.7 %copy-start.6 = (f32[128,64,128]{2,0,1:T(8,128)S(1)}, f32[128,64,128]{2,0,1:T(8,128)}, u32[]{:S(2)}) copy-start(f32[128,64,128]{2,0,1:T(8,128)} %get-tuple-element.19) | copy-start | bytes 12582916
  221.1 44.5 %collective-permute-start.3 = (bf16[128,64,128]{2,1,0:T(8,128)(2,1)}, bf16[128,64,128]{2,1,0:T(8,128)(2,1)}, u32[]{:S(2)}, u32[]{:S(2)}) collective-permute-start(bf16[128,64,128]{2,1,0:T(8,128)(2,1)} %gather_fusion.7), channel_id=1, source_target_pairs={{1,0},{2,1},{3,2},{4,3},{5,4},{6,5},{7,6},{9,8},{10,9},{11,10},{12... | collective-permute-start | bytes 6291464 | tf_op jit(solution)/shard_map/ppermute | solution.py:19
  249.5 10.6 %slice-start.4 = ((s8[4718592]{0:T(1024)(128)(4,1)}), s8[524288]{0:T(1024)(128)(4,1)S(1)}, s32[]{:S(2)}) async-start(s8[4718592]{0:T(1024)(128)(4,1)} %bitcast.84), calls=%async_computation.4 | async-start | bytes 1048576
  253.3 6.8 %slice-start.5 = ((s8[4718592]{0:T(1024)(128)(4,1)}), s8[4194304]{0:T(1024)(128)(4,1)S(1)}, s32[]{:S(2)}) async-start(s8[4718592]{0:T(1024)(128)(4,1)} %bitcast.84), calls=%async_computation.5 | async-start | bytes 8388608
  253.3 6.8 %copy-start.4 = (f32[96,64,128]{2,1,0:T(8,128)S(1)}, f32[96,64,128]{2,1,0:T(8,128)}, u32[]{:S(2)}) copy-start(f32[96,64,128]{2,1,0:T(8,128)} %copy-done.3) | copy-start | bytes 9437188
  260.1 5.6 %copy-start.2 = (f32[128,64,128]{2,1,0:T(8,128)S(1)}, f32[128,64,128]{2,1,0:T(8,128)}, u32[]{:S(2)}) copy-start(f32[128,64,128]{2,1,0:T(8,128)} %copy-done.1) | copy-start | bytes 12582916
  260.1 6.3 %copy-start.8 = (bf16[128,64,128]{2,1,0:T(8,128)(2,1)S(1)}, bf16[128,64,128]{2,1,0:T(8,128)(2,1)}, u32[]{:S(2)}) copy-start(bf16[128,64,128]{2,1,0:T(8,128)(2,1)} %gather_fusion.6) | copy-start | bytes 6291460
where the time goes:
time: 276 us; the launch traced here: 272 us
  matrix products  117 us (42%)
  local copies, waits for them, and re-layouts  80.6 us (29%)
  blocking collectives  34.8 us (13%)
  starting transfers between devices  33.4 us (12%)
  other arithmetic  3.58 us (1%)
    dot_general x6, matrix products, sum_into(): jnp.einsum('bk,kos->bos', selector, terms, precision=lax.Precision.HIGHES...  67.9 us
    psum x2, blocking collectives, body(): lax.psum(grad_part.astype(jnp.bfloat16), 'scen').astype(jnp.float32)  34.8 us
    ppermute x4, starting transfers between devices, from_behind(): return lax.ppermute(value, axis, pairs)  33.4 us
    dot_general x2, local copies, waits for them, and re-layouts, transpose_blocks(): jnp.einsum('roj,ros->rjs', block_mats, dual_rows, preferred_element_type=...  25.5 us
    dot_general x4, matrix products, apply_blocks(): jnp.einsum('roj,rjs->ros', block_mats, stacked, preferred_element_type=jn...  21.9 us
    dot_general x4, matrix products, transpose_blocks(): jnp.einsum('roj,ros->rjs', block_mats, dual_rows, preferred_element_type=...  18.3 us
    unnamed x51, local copies, waits for them, and re-layouts  13 us
    gather x2, local copies, waits for them, and re-layouts, body(): gathered = second_bar[w_pattern].reshape(row_count, lead, scen_dev)  11.3 us
  transfers between devices with their start and end apart: 4, of which 1 were waited for; matrix products, arithmetic and copies ran while one was open for 50% of the time, Pallas kernels for 0%

commit v1 on v0

--- a/solution.py
+++ b/solution.py
@@ -98,7 +98,9 @@
         left_terms = from_behind(tie_terms[:, BLK:], "net", 1)
         grad_second = grad_second + sum_into(right_select, own_terms)
         grad_second = grad_second + sum_into(left_select, left_terms)
-        grad_first = lax.psum(grad_part.astype(jnp.bfloat16), "scen").astype(jnp.float32)
+        grad_first = jnp.sum(
+            lax.all_gather(grad_part.astype(jnp.bfloat16), axis_name="scen"), axis=0
+        ).astype(jnp.float32)
         first_next = jnp.clip(first_now - first_step * (commit_cost - grad_first), 0.0, 1.0)
         second_next = jnp.maximum(second_now - primal_step * (cost_col - grad_second), 0.0)
         first_bar = (2.0 * first_next - first_now).astype(jnp.bfloat16)

time: 276 us -> 266 us (0.964)
  blocking collectives: 34.8 us -> 24.9 us
    psum x2 -> x0, blocking collectives: 34.8 us -> none  [body(): lax.psum(grad_part.astype(jnp.bfloat16), 'scen').astype(jnp.float32)]
    all_gather x0 -> x2, blocking collectives: none -> 24.9 us  [body(): lax.all_gather(grad_part.astype(jnp.bfloat16), axis_name='scen')]
  transfers between devices with their start and end apart: 4 -> 4, of which waited for: 1 -> 1; matrix products, arithmetic and copies ran while one was open for 50% -> 52% of each run, Pallas kernels for 0% -> 0%
where the time goes in v1:
time: 266 us; the launch traced here: 262 us
  matrix products  117 us (44%)
  local copies, waits for them, and re-layouts  80.6 us (30%)
  starting transfers between devices  33.4 us (13%)
  blocking collectives  24.9 us (9%)
  other arithmetic  3.76 us (1%)
    dot_general x6, matrix products, sum_into(): jnp.einsum('bk,kos->bos', selector, terms, precision=lax.Precision.HIGHES...  67.6 us
    ppermute x4, starting transfers between devices, from_behind(): return lax.ppermute(value, axis, pairs)  33.4 us
    dot_general x2, local copies, waits for them, and re-layouts, transpose_blocks(): jnp.einsum('roj,ros->rjs', block_mats, dual_rows, preferred_element_type=...  25.5 us
    all_gather x2, blocking collectives, body(): lax.all_gather(grad_part.astype(jnp.bfloat16), axis_name='scen')  24.9 us
    dot_general x4, matrix products, apply_blocks(): jnp.einsum('roj,rjs->ros', block_mats, stacked, preferred_element_type=jn...  21.9 us
    dot_general x4, matrix products, transpose_blocks(): jnp.einsum('roj,ros->rjs', block_mats, dual_rows, preferred_element_type=...  18.3 us
    unnamed x51, local copies, waits for them, and re-layouts  13 us
    gather x2, local copies, waits for them, and re-layouts, body(): gathered = second_bar[w_pattern].reshape(row_count, lead, scen_dev)  11.3 us
  transfers between devices with their start and end apart: 4, of which 1 were waited for; matrix products, arithmetic and copies ran while one was open for 52% of the time, Pallas kernels for 0%

profile of v1, /device:TPU:0, one launch (start us, length us, event | category | flops | bytes accessed | tf_op | source)
XLA Modules:
  0.0 261.7 jit_solution(14452418326508924166)
XLA Ops:
  0.6 0.0 copy-start
  0.7 1.6 copy-done
  2.2 3.7 %convolution_bitcast_fusion.3 = f32[128,128,128]{2,1,0:T(8,128)S(1)} fusion(bf16[128,64,128]{2,1,0:T(8,128)(2,1)S(1)} %copy-done, f32[128,64,128]{2,1,0:T(8,128)} %param.29, f32[]{:T(128)S(6)} %convert_element_type.69), kind=kOutput, calls=%fused_computation.40 | convolution fusion | flops 270532608 | bytes 14680068 | tf_op jit(solution)/shard_map/roj,ros->rjs/dot_general | solution.py:27
  5.9 0.0 slice-start.1
  5.9 0.0 copy-start.5
  5.9 4.3 %fusion.85 = (f32[128,64,128]{2,1,0:T(8,128)}, f32[128,64,128]{2,1,0:T(8,128)}) fusion(f32[128,128,128]{2,1,0:T(8,128)S(1)} %convolution_bitcast_fusion.3), kind=kLoop, calls=%fused_computation.111 | loop fusion | bytes 16777216 | tf_op jit(solution)/shard_map/slice | solution.py:98
  10.2 4.3 %collective-permute-start = (f32[128,64,128]{2,1,0:T(8,128)}, f32[128,64,128]{2,1,0:T(8,128)}, u32[]{:S(2)}, u32[]{:S(2)}) collective-permute-start(f32[128,64,128]{2,1,0:T(8,128)} %get-tuple-element.24), channel_id=1, source_target_pairs={{0,1},{1,2},{2,3},{3,4},{4,5},{5,6},{6,7},{8,9},{9,10},{10,11},{11... | collective-permute-start | bytes 12582920 | tf_op jit(solution)/shard_map/ppermute | solution.py:19
  15.2 6.9 %convolution_bitcast_fusion.1 = f32[96,256,128]{1,2,0:T(8,128)} fusion(bf16[96,64,320]{2,1,0:T(8,128)(2,1)S(1)} %bitcast.85, f32[96,64,128]{2,1,0:T(8,128)S(1)} %copy-done.5, f32[96]{0:T(128)S(1)} %compare_convert_fusion), kind=kOutput, calls=%fused_computation.13 | convolution fusion | flops 404226048 | bytes 18874880 | tf_op jit(solution)/shard_map/roj,ros->rjs/dot_general | solution.py:27
  22.1 12.8 %copy.88 = f32[96,256,128]{2,1,0:T(8,128)} copy(f32[96,256,128]{1,2,0:T(8,128)} %convolution_bitcast_fusion.1) | data formatting | bytes 25165824 | tf_op jit(solution)/shard_map/roj,ros->rjs/dot_general | solution.py:27
  35.0 0.1 copy.87
  35.1 0.1 eq.57
  35.2 6.7 %fusion.20 = f32[128,64,128]{2,0,1:T(8,128)S(1)} fusion(f32[128,64,128]{2,1,0:T(8,128)} %get-tuple-element.25, s32[128]{0:T(128)S(1)} %copy-done.16), kind=kOutput, calls=%fused_computation.32 | convolution fusion | flops 1610629120 | bytes 8389120 | tf_op jit(solution)/shard_map/bk,kos->bos/dot_general | solution.py:35
  41.9 0.0 copy-start.9
  41.9 16.6 %fusion.2 = f32[128,64,128]{2,0,1:T(8,128)S(1)} fusion(f32[384,64,128]{2,1,0:T(8,128)} %bitcast.82, s32[384]{0:T(512)S(1)} %eq.57), kind=kOutput, calls=%fused_computation.10 | convolution fusion | flops 4831887360 | bytes 16778752 | tf_op jit(solution)/shard_map/bk,kos->bos/dot_general | solution.py:35
  58.6 13.3 %subtract_convert_fusion.1 = (bf16[128,64,128]{2,0,1:T(8,128)(2,1)S(1)}, f32[128,64,128]{2,0,1:T(8,128)}) fusion(f32[128,64,128]{2,1,0:T(8,128)S(1)} %copy-done.9, f32[128,64,128]{2,1,0:T(8,128)} %collective-permute-done, s32[128]{0:T(128)S(1)} %copy-done.15, f32[128,64,128]{2,0,1:T(8,128)S(1)} %fusion.2, f32[128,64,128]{2,0,1:T(8,128)S(1)} %fusion.20, ...), kind=kOutput, calls=%fused_computation.36 | convolution fusion | flops 1620066304 | bytes 23101952 | tf_op jit(solution)/shard_map/bk,kos->bos/dot_general | solution.py:35
  71.9 2.7 %copy.95 = bf16[128,64,128]{2,1,0:T(8,128)(2,1)} copy(bf16[128,64,128]{2,0,1:T(8,128)(2,1)S(1)} %get-tuple-element.26) | data formatting | bytes 4194304 | tf_op jit(solution)/shard_map/convert_element_type | solution.py:107
  74.5 3.7 %gather_fusion.3 = bf16[128,64,128]{2,1,0:T(8,128)(2,1)} fusion(bf16[128,64,128]{2,1,0:T(8,128)(2,1)} %copy.95, s32[1024]{0:T(1024)S(1)} %pad_clamp_fusion), kind=kCustom, calls=%fused_computation.3 | custom fusion | bytes 4194816 | tf_op jit(solution)/shard_map/gather | solution.py:108
  78.3 1.3 collective-permute-start.1
  79.6 2.9 %convert_reduce_fusion.1 = f32[96,64]{1,0:T(8,128)S(1)} fusion(f32[96,64,128]{2,1,0:T(8,128)} %param.28, f32[96]{0:T(128)S(1)} %compare_convert_fusion), kind=kLoop, calls=%fused_computation.51 | loop fusion | flops 3139584 | bytes 3170688 | tf_op jit(solution)/shard_map/roj,ros->rj/reduce_sum | solution.py:87
  82.5 3.7 %gather_fusion.2 = bf16[128,64,128]{2,1,0:T(8,128)(2,1)} fusion(bf16[128,64,128]{2,1,0:T(8,128)(2,1)} %copy.95, s32[1024]{0:T(1024)S(1)} %pad_clamp_fusion.1), kind=kCustom, calls=%fused_computation.2 | custom fusion | bytes 4194816 | tf_op jit(solution)/shard_map/gather | solution.py:109
  86.2 0.3 collective-permute-done.1
  86.5 4.7 %fusion.13 = f32[128,64,128]{2,1,0:T(8,128)S(1)} fusion(f32[128,64,128]{2,1,0:T(8,128)} %param.29, bf16[128,64,128]{2,1,0:T(8,128)(2,1)S(1)} %copy-done, bf16[128,64,128]{2,1,0:T(8,128)(2,1)} %collective-permute-done.1, bf16[128,64,128]{2,1,0:T(8,128)(2,1)} %gather_fusion.2, f32[]{:T(128)S(6)} %convert_element_type.69), kind=kOutput, calls=%fused_computation.25 | convolution fusion | flops 281018368 | bytes 14680068 | tf_op jit(solution)/shard_map/roj,rjs->ros/dot_general | solution.py:23
  91.2 2.0 copy-done.1
  93.2 1.3 convolution_bitcast_fusion.2
  94.5 0.0 copy-start.17
  94.5 0.0 copy-start.11
  94.5 0.0 copy-start.13
  94.5 4.2 %fusion.84 = (f32[128,64,128]{2,1,0:T(8,128)}, f32[128,64,128]{2,1,0:T(8,128)}) fusion(f32[128,128,128]{2,1,0:T(8,128)S(1)} %convolution_bitcast_fusion.2), kind=kLoop, calls=%fused_computation.110 | loop fusion | bytes 16777216 | tf_op jit(solution)/shard_map/slice | solution.py:98
  98.7 26.5 %collective-permute-start.2 = (f32[128,64,128]{2,1,0:T(8,128)}, f32[128,64,128]{2,1,0:T(8,128)}, u32[]{:S(2)}, u32[]{:S(2)}) collective-permute-start(f32[128,64,128]{2,1,0:T(8,128)} %get-tuple-element.22), channel_id=1, source_target_pairs={{0,1},{1,2},{2,3},{3,4},{4,5},{5,6},{6,7},{8,9},{9,10},{10,11},{11... | collective-permute-start | bytes 12582920 | tf_op jit(solution)/shard_map/ppermute | solution.py:19
  125.3 1.9 fusion.54
  127.2 0.2 convolution_convert_fusion.1
  127.4 12.7 %all-gather = bf16[512,64]{0,1:T(8,128)(2,1)S(1)} all-gather(bf16[128,64]{0,1:T(8,128)(2,1)S(1)} %convolution_convert_fusion.1), channel_id=2, replica_groups=mesh['scen'=4,'net'=8] {'scen'}, dimensions={0}, use_global_device_ids=true | all-gather | bytes 81920 | tf_op jit(solution)/shard_map/all_gather | solution.py:102
  140.1 0.1 reduce_sum.43
  140.2 0.1 copy.96
  140.4 0.1 copy.94
  140.5 0.1 reshape.39
  140.6 0.1 copy.86
  140.7 0.7 gather_fusion.1
  141.4 2.3 fusion.52
  143.7 5.7 %gather_fusion = bf16[384,64,128]{2,1,0:T(8,128)(2,1)} fusion(bf16[128,64,128]{2,1,0:T(8,128)(2,1)} %copy.95, s32[1024]{0:T(1024)S(1)} %pad_clamp_fusion.3), kind=kCustom, calls=%fused_computation | custom fusion | bytes 12584448 | tf_op jit(solution)/shard_map/gather | solution.py:111
  149.4 6.8 %convert_reduce_fusion = (f32[96,64]{1,0:T(8,128)S(1)}, f32[96,64,128]{2,1,0:T(8,128)S(1)}) fusion(f32[96,64]{1,0:T(8,128)S(1)} %bitcast.97, bf16[96,256,128]{2,1,0:T(8,128)(2,1)} %bitcast.91, bf16[96,64,320]{2,1,0:T(8,128)(2,1)} %param.15, bf16[96,64,128]{2,1,0:T(8,128)(2,1)} %param.25, f32[96,64]{1,0:T(8,128)S(1)} %copy.86, f32[96,64,128]{2,1,0:T(8,128)} %param.28, ...), kind=kOutput, calls=%fused_computation.49 | convolution fusion | flops 411297792 | bytes 17375616 | tf_op jit(solution)/shard_map/roj,rjs->ros/dot_general | solution.py:23
  156.2 1.7 copy-done.3
  157.8 6.4 %convolution_bitcast_fusion = f32[96,256,128]{1,2,0:T(8,128)} fusion(bf16[96,64,320]{2,1,0:T(8,128)(2,1)S(1)} %bitcast.87, f32[96,64,128]{2,1,0:T(8,128)S(1)} %get-tuple-element.29), kind=kOutput, calls=%fused_computation.12 | convolution fusion | flops 403439616 | bytes 18874368 | tf_op jit(solution)/shard_map/roj,ros->rjs/dot_general | solution.py:27
  164.2 12.6 %copy.97 = f32[96,256,128]{2,1,0:T(8,128)} copy(f32[96,256,128]{1,2,0:T(8,128)} %convolution_bitcast_fusion) | data formatting | bytes 25165824 | tf_op jit(solution)/shard_map/roj,ros->rjs/dot_general | solution.py:27
  176.9 16.8 %fusion = f32[128,64,128]{2,0,1:T(8,128)S(1)} fusion(f32[384,64,128]{2,1,0:T(8,128)} %bitcast.83, s32[384]{0:T(512)S(1)} %eq.57), kind=kOutput, calls=%fused_computation.8 | convolution fusion | flops 4831887360 | bytes 16778752 | tf_op jit(solution)/shard_map/bk,kos->bos/dot_general | solution.py:35
  193.7 4.7 %fusion.16 = f32[128,64,128]{2,0,1:T(8,128)S(1)} fusion(f32[128,64,128]{2,1,0:T(8,128)S(1)} %copy-done.7, s32[128]{0:T(128)S(1)} %copy-done.16), kind=kOutput, calls=%fused_computation.28 | convolution fusion | flops 1610629120 | bytes 8389120 | tf_op jit(solution)/shard_map/bk,kos->bos/dot_general | solution.py:35
  198.4 9.6 %subtract_convert_fusion = (bf16[128,64,128]{2,0,1:T(8,128)(2,1)S(1)}, f32[128,64,128]{2,0,1:T(8,128)}) fusion(f32[128,64,128]{2,0,1:T(8,128)S(1)} %copy-done.6, f32[128,64,128]{2,1,0:T(8,128)} %collective-permute-done.2, s32[128]{0:T(128)S(1)} %copy-done.15, f32[128,64,128]{2,0,1:T(8,128)S(1)} %fusion, f32[128,64,128]{2,0,1:T(8,128)S(1)} %fusion.16, ...), kind=kOutput, calls=%fused_computation.34 | convolution fusion | flops 1620066304 | bytes 23101952 | tf_op jit(solution)/shard_map/bk,kos->bos/dot_general | solution.py:35
  208.0 2.7 %copy.103 = bf16[128,64,128]{2,1,0:T(8,128)(2,1)} copy(bf16[128,64,128]{2,0,1:T(8,128)(2,1)S(1)} %get-tuple-element.30) | data formatting | bytes 4194304 | tf_op jit(solution)/shard_map/convert_element_type | solution.py:107
  210.6 3.8 %gather_fusion.7 = bf16[128,64,128]{2,1,0:T(8,128)(2,1)} fusion(bf16[128,64,128]{2,1,0:T(8,128)(2,1)} %copy.103, s32[1024]{0:T(1024)S(1)} %pad_clamp_fusion), kind=kCustom, calls=%fused_computation.7 | custom fusion | bytes 4194816 | tf_op jit(solution)/shard_map/gather | solution.py:108
  214.4 1.3 collective-permute-start.3
  215.7 1.9 fusion.50
  217.6 0.2 convolution_convert_fusion
  217.9 12.2 %all-gather.1 = bf16[512,64]{0,1:T(8,128)(2,1)S(1)} all-gather(bf16[128,64]{0,1:T(8,128)(2,1)S(1)} %convolution_convert_fusion), channel_id=3, replica_groups=mesh['scen'=4,'net'=8] {'scen'}, dimensions={0}, use_global_device_ids=true | all-gather | bytes 81920 | tf_op jit(solution)/shard_map/all_gather | solution.py:102
  230.2 0.1 reduce_sum.45
  230.2 0.6 subtract_convert_fusion.2
  230.9 0.1 copy.104
  231.0 0.7 gather_fusion.5
  231.7 2.3 fusion.48
  234.0 5.6 %gather_fusion.4 = bf16[384,64,128]{2,1,0:T(8,128)(2,1)} fusion(bf16[128,64,128]{2,1,0:T(8,128)(2,1)} %copy.103, s32[1024]{0:T(1024)S(1)} %pad_clamp_fusion.3), kind=kCustom, calls=%fused_computation.4 | custom fusion | bytes 12584448 | tf_op jit(solution)/shard_map/gather | solution.py:111
  239.6 3.8 %gather_fusion.6 = bf16[128,64,128]{2,1,0:T(8,128)(2,1)} fusion(bf16[128,64,128]{2,1,0:T(8,128)(2,1)} %copy.103, s32[1024]{0:T(1024)S(1)} %pad_clamp_fusion.1), kind=kCustom, calls=%fused_computation.6 | custom fusion | bytes 4194816 | tf_op jit(solution)/shard_map/gather | solution.py:109
  243.4 6.8 %copy.107 = f32[128,64,128]{2,1,0:T(8,128)} copy(f32[128,64,128]{2,0,1:T(8,128)} %get-tuple-element.31) | data formatting | bytes 8388608
  250.3 5.5 %fusion.24 = f32[96,64,128]{2,1,0:T(8,128)} fusion(f32[96,64,128]{2,1,0:T(8,128)S(1)} %copy-done.4, bf16[96,64,128]{2,1,0:T(8,128)(2,1)} %param.25, bf16[96,256,128]{2,1,0:T(8,128)(2,1)} %bitcast.90, bf16[96,64,320]{2,1,0:T(8,128)(2,1)S(1)} %bitcast.89, f32[96,64]{1,0:T(8,128)S(1)} %bitcast.92, f32[96,64]{1,0:T(8,128)S(1)} %copy.86, ...), kind=kOutput, calls=%fused_computation.44 | convolution fusion | flops 408158208 | bytes 17400320 | tf_op jit(solution)/shard_map/roj,rjs->ros/dot_general | solution.py:23
  255.8 0.7 copy-done.8
  256.5 4.9 %fusion.12 = f32[128,64,128]{2,1,0:T(8,128)} fusion(f32[128,64,128]{2,1,0:T(8,128)S(1)} %copy-done.2, bf16[128,64,128]{2,1,0:T(8,128)(2,1)S(1)} %copy-done, bf16[128,64,128]{2,1,0:T(8,128)(2,1)} %collective-permute-done.3, bf16[128,64,128]{2,1,0:T(8,128)(2,1)S(1)} %copy-done.8, f32[]{:T(128)S(6)} %convert_element_type.69), kind=kOutput, calls=%fused_computation.23 | convolution fusion | flops 279969792 | bytes 14680068 | tf_op jit(solution)/shard_map/roj,rjs->ros/dot_general | solution.py:23
  (55 shorter events, 0.2 us)
Async XLA Ops:
  0.6 1.6 copy-start
  2.2 13.0 %slice-start = ((s8[4718592]{0:T(1024)(128)(4,1)}), s8[4194304]{0:T(1024)(128)(4,1)S(1)}, s32[]{:S(2)}) async-start(s8[4718592]{0:T(1024)(128)(4,1)} %bitcast.84), calls=%async_computation | async-start | bytes 8388608
  5.9 9.3 %slice-start.1 = ((s8[4718592]{0:T(1024)(128)(4,1)}), s8[524288]{0:T(1024)(128)(4,1)S(1)}, s32[]{:S(2)}) async-start(s8[4718592]{0:T(1024)(128)(4,1)} %bitcast.84), calls=%async_computation.1 | async-start | bytes 1048576
  5.9 9.3 %copy-start.5 = (f32[96,64,128]{2,1,0:T(8,128)S(1)}, f32[96,64,128]{2,1,0:T(8,128)}, u32[]{:S(2)}) copy-start(f32[96,64,128]{2,1,0:T(8,128)} %param.28) | copy-start | bytes 9437188
  10.2 48.3 %collective-permute-start = (f32[128,64,128]{2,1,0:T(8,128)}, f32[128,64,128]{2,1,0:T(8,128)}, u32[]{:S(2)}, u32[]{:S(2)}) collective-permute-start(f32[128,64,128]{2,1,0:T(8,128)} %get-tuple-element.24), channel_id=1, source_target_pairs={{0,1},{1,2},{2,3},{3,4},{4,5},{5,6},{6,7},{8,9},{9,10},{10,11},{11... | collective-permute-start | bytes 12582920 | tf_op jit(solution)/shard_map/ppermute | solution.py:19
  22.1 12.8 %copy-start.14 = (s32[96,4]{0,1:T(4,128)S(1)}, s32[96,4]{0,1:T(4,128)}, u32[]{:S(2)}) copy-start(s32[96,4]{0,1:T(4,128)} %param.17) | copy-start | bytes 4612
  22.1 13.0 %copy-start.15 = (s32[128]{0:T(128)S(1)}, s32[128]{0:T(128)}, u32[]{:S(2)}) copy-start(s32[128]{0:T(128)} %param.19) | copy-start | bytes 1540
  22.1 13.1 %copy-start.16 = (s32[128]{0:T(128)S(1)}, s32[128]{0:T(128)}, u32[]{:S(2)}) copy-start(s32[128]{0:T(128)} %param.20) | copy-start | bytes 1540
  41.9 16.7 %copy-start.9 = (f32[128,64,128]{2,1,0:T(8,128)S(1)}, f32[128,64,128]{2,1,0:T(8,128)}, u32[]{:S(2)}) copy-start(f32[128,64,128]{2,1,0:T(8,128)} %param.27) | copy-start | bytes 12582916
  41.9 16.7 %copy-start.10 = (f32[128,64]{0,1:T(8,128)S(1)}, f32[128,64]{0,1:T(8,128)}, u32[]{:S(2)}) copy-start(f32[128,64]{0,1:T(8,128)} %param.23) | copy-start | bytes 98308
  78.3 8.2 %collective-permute-start.1 = (bf16[128,64,128]{2,1,0:T(8,128)(2,1)}, bf16[128,64,128]{2,1,0:T(8,128)(2,1)}, u32[]{:S(2)}, u32[]{:S(2)}) collective-permute-start(bf16[128,64,128]{2,1,0:T(8,128)(2,1)} %gather_fusion.3), channel_id=1, source_target_pairs={{1,0},{2,1},{3,2},{4,3},{5,4},{6,5},{7,6},{9,8},{10,9},{11,10},{12... | collective-permute-start | bytes 6291464 | tf_op jit(solution)/shard_map/ppermute | solution.py:19
  91.2 2.0 copy-start.1
  94.5 32.7 %copy-start.17 = (s32[96]{0:T(128)S(1)}, s32[96]{0:T(128)}, u32[]{:S(2)}) copy-start(s32[96]{0:T(128)} %param.18) | copy-start | bytes 1156
  94.5 45.7 %copy-start.11 = (f32[128,64]{0,1:T(8,128)S(1)}, f32[128,64]{0,1:T(8,128)}, u32[]{:S(2)}) copy-start(f32[128,64]{0,1:T(8,128)} %param.26) | copy-start | bytes 98308
  94.5 45.7 %copy-start.12 = (f32[128,64]{0,1:T(8,128)S(1)}, f32[128,64]{0,1:T(8,128)}, u32[]{:S(2)}) copy-start(f32[128,64]{0,1:T(8,128)} %param.22) | copy-start | bytes 98308
  94.5 46.1 %copy-start.13 = (f32[96,64]{0,1:T(8,128)S(1)}, f32[96,64]{0,1:T(8,128)}, u32[]{:S(2)}) copy-start(f32[96,64]{0,1:T(8,128)} %param.24) | copy-start | bytes 73732
  98.7 99.6 %collective-permute-start.2 = (f32[128,64,128]{2,1,0:T(8,128)}, f32[128,64,128]{2,1,0:T(8,128)}, u32[]{:S(2)}, u32[]{:S(2)}) collective-permute-start(f32[128,64,128]{2,1,0:T(8,128)} %get-tuple-element.22), channel_id=1, source_target_pairs={{0,1},{1,2},{2,3},{3,4},{4,5},{5,6},{6,7},{8,9},{9,10},{10,11},{11... | collective-permute-start | bytes 12582920 | tf_op jit(solution)/shard_map/ppermute | solution.py:19
  143.7 14.1 %slice-start.2 = ((s8[4718592]{0:T(1024)(128)(4,1)}), s8[524288]{0:T(1024)(128)(4,1)S(1)}, s32[]{:S(2)}) async-start(s8[4718592]{0:T(1024)(128)(4,1)} %bitcast.86), calls=%async_computation.2 | async-start | bytes 1048576
  149.4 8.4 %slice-start.3 = ((s8[4718592]{0:T(1024)(128)(4,1)}), s8[4194304]{0:T(1024)(128)(4,1)S(1)}, s32[]{:S(2)}) async-start(s8[4718592]{0:T(1024)(128)(4,1)} %bitcast.86), calls=%async_computation.3 | async-start | bytes 8388608
  156.1 1.7 copy-start.3
  176.9 16.8 %copy-start.7 = (f32[128,64,128]{2,1,0:T(8,128)S(1)}, f32[128,64,128]{2,1,0:T(8,128)}, u32[]{:S(2)}) copy-start(f32[128,64,128]{2,1,0:T(8,128)} %get-tuple-element.23) | copy-start | bytes 12582916
  193.7 4.7 %copy-start.6 = (f32[128,64,128]{2,0,1:T(8,128)S(1)}, f32[128,64,128]{2,0,1:T(8,128)}, u32[]{:S(2)}) copy-start(f32[128,64,128]{2,0,1:T(8,128)} %get-tuple-element.27) | copy-start | bytes 12582916
  214.4 41.4 %collective-permute-start.3 = (bf16[128,64,128]{2,1,0:T(8,128)(2,1)}, bf16[128,64,128]{2,1,0:T(8,128)(2,1)}, u32[]{:S(2)}, u32[]{:S(2)}) collective-permute-start(bf16[128,64,128]{2,1,0:T(8,128)(2,1)} %gather_fusion.7), channel_id=1, source_target_pairs={{1,0},{2,1},{3,2},{4,3},{5,4},{6,5},{7,6},{9,8},{10,9},{11,10},{12... | collective-permute-start | bytes 6291464 | tf_op jit(solution)/shard_map/ppermute | solution.py:19
  239.6 10.6 %slice-start.4 = ((s8[4718592]{0:T(1024)(128)(4,1)}), s8[524288]{0:T(1024)(128)(4,1)S(1)}, s32[]{:S(2)}) async-start(s8[4718592]{0:T(1024)(128)(4,1)} %bitcast.88), calls=%async_computation.4 | async-start | bytes 1048576
  243.4 6.8 %slice-start.5 = ((s8[4718592]{0:T(1024)(128)(4,1)}), s8[4194304]{0:T(1024)(128)(4,1)S(1)}, s32[]{:S(2)}) async-start(s8[4718592]{0:T(1024)(128)(4,1)} %bitcast.88), calls=%async_computation.5 | async-start | bytes 8388608
  243.4 6.8 %copy-start.4 = (f32[96,64,128]{2,1,0:T(8,128)S(1)}, f32[96,64,128]{2,1,0:T(8,128)}, u32[]{:S(2)}) copy-start(f32[96,64,128]{2,1,0:T(8,128)} %copy-done.3) | copy-start | bytes 9437188
  250.2 5.6 %copy-start.2 = (f32[128,64,128]{2,1,0:T(8,128)S(1)}, f32[128,64,128]{2,1,0:T(8,128)}, u32[]{:S(2)}) copy-start(f32[128,64,128]{2,1,0:T(8,128)} %copy-done.1) | copy-start | bytes 12582916
  250.2 6.3 %copy-start.8 = (bf16[128,64,128]{2,1,0:T(8,128)(2,1)S(1)}, bf16[128,64,128]{2,1,0:T(8,128)(2,1)}, u32[]{:S(2)}) copy-start(bf16[128,64,128]{2,1,0:T(8,128)(2,1)} %gather_fusion.6) | copy-start | bytes 6291460
